TPU v7x, 128 devices: a whole 4x4x4 slice. The times are simulated.
128 devices in a mesh: row: 16 (over y_lo, z, core), col: 8 (over y_hi, x).
Axes of the slice: x: 4, y: 4 (y_hi: 2, y_lo: 2; y = y_hi * 2 + y_lo), z: 4, core: 2. Of those that a mesh axis runs over, the one named last changes fastest.
Arguments:
- features: bfloat16 [65536, 512], P(('row', 'col')), may hold values from -6 to 6
- partition_of: int32 [65536], P(('row', 'col')), may hold values from 0 to 127, as said below
- weight: bfloat16 [512, 512], replicated, may hold values from -0.25 to 0.25
- tile_values: bfloat16 [16, 8, 192, 128, 128], P('row', 'col'), may hold values from -0.109375 to 0.109375
- tile_rows: int32 [16, 8, 192], P('row', 'col'), may hold values from 0 to 31
- tile_cols: int32 [16, 8, 192], P('row', 'col'), may hold values from 0 to 63
- tile_count: int32 [16, 8], P('row', 'col'), may hold values from 48 to 192, as said below
- out_cotangent: bfloat16 [65536, 512], P('row'), may hold values from -6 to 6
Outputs:
- activations: bfloat16 [65536, 512], P(('row', 'col'))
- weight_grad: float32 [512, 512], replicated
Inputs may be any that keep to these rules, and one draw needn't show every extreme that they name: `partition_of`: of the 512 regions of each device in detection order, exactly 4 go to each partition. `tile_count`: some grid position has all 192 slots live in every draw.
All inputs are finite; a program needn't handle non-finite values.
Results may differ from a plain program's by a relative error of at most 0.005.
Values may be sent and summed in bfloat16 or wider, within the bound.
No kernel may reach another device: no remote copies, remote signals or barrier semaphores. Data moves between devices by JAX's collectives and lax.ppermute only.
A program may use at most 192 MiB of HBM per device.

v0:
```python
import math
import jax
import jax.numpy as jnp
from jax import lax
from jax.sharding import PartitionSpec as P


def silu_slope(pre):
    sigmoid = jax.nn.sigmoid(pre)
    return sigmoid * (1.0 + pre * (1.0 - sigmoid))


def regroup(features, partition_of, n_row, n_col):
    slots, feature_width = features.shape
    per_peer = slots // (n_row * n_col)
    ordering = jnp.argsort(partition_of, stable=True)
    outgoing = features[ordering]
    shaped = outgoing.reshape(n_row * n_col, per_peer, feature_width)
    arrived = lax.all_to_all(shaped, ("row", "col"), split_axis=0, concat_axis=0, tiled=True)
    return arrived.reshape(slots, feature_width)


def tile_products(blocks, row_index, column_index, live_count, sources, out_tiles, forward):
    tile_size = blocks.shape[-1]
    feature_width = sources.shape[-1]
    source_tiles = sources.reshape(-1, tile_size, feature_width)
    empty = jnp.zeros((out_tiles, tile_size, feature_width), jnp.float32)
    block_total = (live_count + 31) // 32

    def one_block(block_step, totals):
        first_slot = block_step * 32
        tile_block = lax.dynamic_slice_in_dim(blocks, first_slot, 32, 0)
        row_part = lax.dynamic_slice_in_dim(row_index, first_slot, 32, 0)
        column_part = lax.dynamic_slice_in_dim(column_index, first_slot, 32, 0)
        is_live = first_slot + jnp.arange(32, dtype=jnp.int32) < live_count
        tile_block = jnp.where(is_live[:, None, None], tile_block, jnp.zeros_like(tile_block))
        if forward:
            picked = source_tiles[column_part]
            products = jnp.einsum(
                "tij,tjf->tif", tile_block, picked, preferred_element_type=jnp.float32
            )
            return totals.at[row_part].add(products)
        picked = source_tiles[row_part]
        products = jnp.einsum(
            "tij,tif->tjf", tile_block, picked, preferred_element_type=jnp.float32
        )
        return totals.at[column_part].add(products)

    totals = lax.fori_loop(0, block_total, one_block, empty)
    return totals.reshape(out_tiles * tile_size, feature_width)


def shards(
    features, partition_of, weight, tile_values, tile_rows, tile_cols, tile_count, out_cotangent
):
    n_row = lax.axis_size("row")
    n_col = lax.axis_size("col")
    regrouped = regroup(features, partition_of, n_row, n_col)
    slots, feature_width = regrouped.shape
    tile_size = tile_values.shape[-1]
    blocks = tile_values.reshape(-1, tile_size, tile_size)
    row_index = tile_rows.reshape(-1)
    column_index = tile_cols.reshape(-1)
    live_count = tile_count.reshape(())
    row_tiles = slots * n_col // tile_size
    column_tiles = slots * n_row // tile_size
    hidden = jnp.dot(regrouped, weight, preferred_element_type=jnp.float32).astype(jnp.bfloat16)
    hidden_columns = lax.all_gather(hidden, "row", axis=0, tiled=True)
    partial_value = tile_products(
        blocks, row_index, column_index, live_count, hidden_columns, row_tiles, True
    )
    position = lax.axis_index("col") * slots
    pre = lax.psum(partial_value, "col")
    own_pre = lax.dynamic_slice_in_dim(pre, position, slots, 0)
    activations = jax.nn.silu(own_pre).astype(jnp.bfloat16)
    slope = (out_cotangent.astype(jnp.float32) * silu_slope(pre)).astype(jnp.bfloat16)
    back_partial = tile_products(
        blocks, row_index, column_index, live_count, slope, column_tiles, False
    )
    hidden_grad = lax.psum_scatter(back_partial, "row", scatter_dimension=0, tiled=True)
    local_grad = jnp.dot(
        regrouped.astype(jnp.float32).T,
        hidden_grad,
        precision=lax.Precision.HIGHEST,
        preferred_element_type=jnp.float32,
    )
    weight_grad = lax.psum(local_grad, ("row", "col")) * (1.0 / math.sqrt(slots * n_row * n_col))
    return (activations, weight_grad)


def solution(mesh):
    placed = (
        P(("row", "col"), None),
        P(("row", "col")),
        P(),
        P("row", "col", None, None, None),
        P("row", "col", None),
        P("row", "col", None),
        P("row", "col"),
        P("row", None),
    )
    return jax.shard_map(
        shards,
        mesh=mesh,
        in_specs=placed,
        out_specs=(P(("row", "col"), None), P()),
        check_vma=False,
    )
```

profile of v0, /device:TPU:1, one launch (start us, length us, event | category | flops | bytes accessed | tf_op | source)
XLA Modules:
  0.0 937.0 jit_solution(18352285362092890931)
XLA Ops:
  13.9 23.8 %all_to_all.5 = bf16[128,4,512]{2,1,0:T(4,128)(2,1)S(1)} all-to-all(bf16[128,4,512]{2,1,0:T(4,128)(2,1)S(1)} %reshape.48), channel_id=1, replica_groups=mesh['row'=16,'col'=8] {'row','col'}, dimensions={0} | all-to-all | bytes 1048576 | tf_op jit(solution)/shard_map/all_to_all | solution.py:19
  41.1 49.4 %all-gather.2.cloned.1.call-done = bf16[8192,512]{1,0:T(8,128)(2,1)} async-done(((bf16[512,512]{1,0:T(8,128)(2,1)}), bf16[8192,512]{1,0:T(8,128)(2,1)}) %all-gather.2.cloned.1.call-update) | async-done | bytes 8388624 | tf_op jit(solution)/shard_map/all_gather | solution.py:68
  94.8 97.0 %while.20 = (s32[]{:T(128)}, f32[32,128,512]{2,1,0:T(8,128)}, s32[]{:T(128)}, s32[192]{0:T(256)S(1)}, s32[]{:T(128)}, /*index=5*/bf16[192,128,128]{2,1,0:T(8,128...) while((s32[]{:T(128)}, f32[32,128,512]{2,1,0:T(8,128)}, ...), condition=%wide.region_3.4_spmd, body=%wide.region_1.3_spmd.sunk | while | flops 539493632 | bytes 47191152 | solution.py:49
  95.6 6.1 gather_fusion
  101.7 7.0 fusion.29
  108.7 18.8 %scatter_fusion = f32[32,128,512]{2,1,0:T(8,128)} fusion(f32[32,128,512]{2,1,0:T(8,128)} %get-tuple-element.257, s32[32]{0:T(128)S(1)} %get-tuple-element.232, f32[32,128,512]{2,1,0:T(8,128)} %fusion.29), kind=kCustom, calls=%fused_computation.3.clone.1 | custom fusion | flops 2097152 | bytes 25165952 | tf_op jit(solution)/shard_map/while/body/scatter-add | solution.py:42
  128.3 6.1 gather_fusion
  134.4 7.0 fusion.29
  141.4 18.5 %scatter_fusion = f32[32,128,512]{2,1,0:T(8,128)} fusion(f32[32,128,512]{2,1,0:T(8,128)} %get-tuple-element.257, s32[32]{0:T(128)S(1)} %get-tuple-element.232, f32[32,128,512]{2,1,0:T(8,128)} %fusion.29), kind=kCustom, calls=%fused_computation.3.clone.1 | custom fusion | flops 2097152 | bytes 25165952 | tf_op jit(solution)/shard_map/while/body/scatter-add | solution.py:42
  166.7 7.0 fusion.29
  173.7 18.1 %scatter_fusion = f32[32,128,512]{2,1,0:T(8,128)} fusion(f32[32,128,512]{2,1,0:T(8,128)} %get-tuple-element.257, s32[32]{0:T(128)S(1)} %get-tuple-element.232, f32[32,128,512]{2,1,0:T(8,128)} %fusion.29), kind=kCustom, calls=%fused_computation.3.clone.1 | custom fusion | flops 2097152 | bytes 25165952 | tf_op jit(solution)/shard_map/while/body/scatter-add | solution.py:42
  191.9 8.6 copy.10
  200.5 275.5 %all-reduce.3.cloned.1.call-done = f32[4096,512]{1,0:T(8,128)} async-done(((f32[4096,512]{1,0:T(8,128)}), f32[4096,512]{1,0:T(8,128)}) %all-reduce.3.cloned.1.call-update) | async-done | bytes 8388624 | tf_op jit(solution)/shard_map/psum | solution.py:73
  476.0 7.6 multiply_convert_fusion
  483.7 7.9 broadcast_in_dim.38
  491.5 94.5 %while.21 = (s32[]{:T(128)}, f32[64,128,512]{2,1,0:T(8,128)}, s32[]{:T(128)}, s32[192]{0:T(256)S(1)}, s32[]{:T(128)}, /*index=5*/bf16[192,128,128]{1,2,0:T(8,128...) while((s32[]{:T(128)}, f32[64,128,512]{2,1,0:T(8,128)}, ...), condition=%wide.region_7.8_spmd, body=%wide.region_5.7_spmd.sunk | while | flops 539493632 | bytes 47191152 | solution.py:49
  497.4 7.0 fusion.32
  504.4 18.6 %scatter_fusion.1 = f32[64,128,512]{2,1,0:T(8,128)} fusion(f32[64,128,512]{2,1,0:T(8,128)} %get-tuple-element.293, s32[32]{0:T(128)S(1)} %get-tuple-element.242, f32[32,128,512]{2,1,0:T(8,128)} %fusion.32), kind=kCustom, calls=%fused_computation.4.clone.1 | custom fusion | flops 2097152 | bytes 25165952 | tf_op jit(solution)/shard_map/while/body/scatter-add | solution.py:47
  528.8 7.0 fusion.32
  535.8 18.6 %scatter_fusion.1 = f32[64,128,512]{2,1,0:T(8,128)} fusion(f32[64,128,512]{2,1,0:T(8,128)} %get-tuple-element.293, s32[32]{0:T(128)S(1)} %get-tuple-element.242, f32[32,128,512]{2,1,0:T(8,128)} %fusion.32), kind=kCustom, calls=%fused_computation.4.clone.1 | custom fusion | flops 2097152 | bytes 25165952 | tf_op jit(solution)/shard_map/while/body/scatter-add | solution.py:47
  560.3 7.0 fusion.32
  567.3 18.7 %scatter_fusion.1 = f32[64,128,512]{2,1,0:T(8,128)} fusion(f32[64,128,512]{2,1,0:T(8,128)} %get-tuple-element.293, s32[32]{0:T(128)S(1)} %get-tuple-element.242, f32[32,128,512]{2,1,0:T(8,128)} %fusion.32), kind=kCustom, calls=%fused_computation.4.clone.1 | custom fusion | flops 2097152 | bytes 25165952 | tf_op jit(solution)/shard_map/while/body/scatter-add | solution.py:47
  586.1 189.1 %reduce-scatter.2.cloned.1.call-done = f32[512,512]{1,0:T(8,128)} async-done(((f32[8192,512]{1,0:T(8,128)}), f32[512,512]{1,0:T(8,128)}) %reduce-scatter.2.cloned.1.call-update) | async-done | bytes 1048592 | tf_op jit(solution)/shard_map/reduce_scatter | solution.py:80
  780.8 147.3 %all-reduce.5.cloned.1.call-done = f32[512,512]{1,0:T(8,128)} async-done(((f32[512,512]{1,0:T(8,128)}), f32[512,512]{1,0:T(8,128)}) %all-reduce.5.cloned.1.call-update) | async-done | bytes 1048592 | tf_op jit(solution)/shard_map/psum | solution.py:87
  (54 shorter events, 47.4 us)
Async XLA Ops:
  7.2 4.6 copy-start
  7.2 83.3 %all-gather.2.cloned.1.call-start = ((), (), s32[]{:S(2)}) async-start(), calls=%async_computation.2 | async-start | bytes 8912896 | tf_op jit(solution)/shard_map/all_gather | solution.py:68
  11.7 83.0 %copy-start.4 = (s32[1,1,192]{2,1,0:T(1,128)S(1)}, s32[1,1,192]{2,1,0:T(1,128)}, u32[]{:S(2)}) copy-start(s32[1,1,192]{2,1,0:T(1,128)} %param.16) | copy-start | bytes 2308
  11.8 83.0 %copy-start.5 = (s32[1,1,192]{2,1,0:T(1,128)S(1)}, s32[1,1,192]{2,1,0:T(1,128)}, u32[]{:S(2)}) copy-start(s32[1,1,192]{2,1,0:T(1,128)} %param.17) | copy-start | bytes 2308
  37.9 56.9 %copy-start.2 = (bf16[512,512]{1,0:T(8,128)(2,1)}, bf16[512,512]{1,0:T(8,128)(2,1)S(1)}, u32[]{:S(2)}) copy-start(bf16[512,512]{1,0:T(8,128)(2,1)S(1)} %reshape.49) | copy-start | bytes 1572868
  40.4 435.7 %all-reduce.3.cloned.1.call-start = ((), (), s32[]{:S(2)}) async-start(), calls=%async_computation.3 | async-start | bytes 16777216 | tf_op jit(solution)/shard_map/psum | solution.py:73
  191.8 583.4 %reduce-scatter.2.cloned.1.call-start = ((), (), s32[]{:S(2)}) async-start(), calls=%async_computation.4 | async-start | bytes 17825792 | tf_op jit(solution)/shard_map/reduce_scatter | solution.py:80
  586.0 344.4 %copy-start.1 = (bf16[512,512]{1,0:T(8,128)(2,1)S(1)}, bf16[512,512]{1,0:T(8,128)(2,1)}, u32[]{:S(2)}) copy-start(bf16[512,512]{1,0:T(8,128)(2,1)} %param.12) | copy-start | bytes 1572868
  586.0 189.2 %copy-start.3 = (bf16[512,512]{1,0:T(8,128)(2,1)S(1)}, bf16[512,512]{1,0:T(8,128)(2,1)}, u32[]{:S(2)}) copy-start(bf16[512,512]{1,0:T(8,128)(2,1)} %copy-done.2) | copy-start | bytes 1572868
  586.1 342.1 %all-reduce.5.cloned.1.call-start = ((), (), s32[]{:S(2)}) async-start(), calls=%async_computation.5 | async-start | bytes 2097152 | tf_op jit(solution)/shard_map/psum | solution.py:87
Sparse Core Ops, SparseCore 0:
  40.5 49.9 all-gather.1
  192.0 284.0 all-reduce.2
  586.2 188.9 reduce-scatter.1
  780.4 147.6 all-reduce.4
where the time goes:
time: 939 us; the launch traced here: 937 us
  waiting for transfers between devices  661 us (70%)
  other arithmetic  132 us (14%)
  local copies, waits for them, and re-layouts  56.7 us (6%)
  matrix products  47.8 us (5%)
  blocking collectives  23.8 us (3%)
  between operations  14.5 us (2%)
    psum x1, waiting for transfers between devices, shards(): pre = lax.psum(partial_value, 'col')  276 us
    reduce_scatter x1, waiting for transfers between devices, shards(): lax.psum_scatter(back_partial, 'row', scatter_dimension=0, tiled=True)  189 us
    psum x1, waiting for transfers between devices, shards(): lax.psum(local_grad, ('row', 'col'))  147 us
    scatter-add x3, other arithmetic, one_block(): return totals.at[column_part].add(products)  55.9 us
    scatter-add x3, other arithmetic, one_block(): return totals.at[row_part].add(products)  55.4 us
    all_gather x1, waiting for transfers between devices, shards(): hidden_columns = lax.all_gather(hidden, 'row', axis=0, tiled=True)  49.4 us
    all_to_all x1, blocking collectives, regroup(): lax.all_to_all(shaped, ('row', 'col'), split_axis=0, concat_axis=0, tiled...  23.8 us
    dot_general x3, matrix products, one_block(): jnp.einsum('tij,tjf->tif', tile_block, picked, preferred_element_type=jnp...  21.1 us
  transfers between devices with their start and end apart: 4, of which 4 were waited for; matrix products, arithmetic and copies ran while one was open for 1% of the time, Pallas kernels for 0%

commit v1 on v0

--- a/solution.py
+++ b/solution.py
@@ -84,7 +84,9 @@
         precision=lax.Precision.HIGHEST,
         preferred_element_type=jnp.float32,
     )
-    weight_grad = lax.psum(local_grad, ("row", "col")) * (1.0 / math.sqrt(slots * n_row * n_col))
+    weight_grad = jnp.sum(lax.all_gather(local_grad, ("row", "col")), axis=0) * (
+        1.0 / math.sqrt(slots * n_row * n_col)
+    )
     return (activations, weight_grad)
 
 

time: 939 us -> 1560 us (1.66)
  waiting for transfers between devices: 661 us -> 1240 us
  other arithmetic: 132 us -> 172 us
    all_gather x0 -> x1, waiting for transfers between devices: none -> 728 us  [shards(): lax.all_gather(local_grad, ('row', 'col'))]
    psum x1 -> x0, waiting for transfers between devices: 147 us -> none  [shards(): lax.psum(local_grad, ('row', 'col'))]
    reduce_sum x0 -> x1, other arithmetic: none -> 40.6 us  [shards(): jnp.sum(lax.all_gather(local_grad, ('row', 'col')), axis=0)]
where the time goes in v1:
time: 1560 us
  waiting for transfers between devices  1240 us (79%)
  other arithmetic  172 us (11%)
  local copies, waits for them, and re-layouts  56.4 us (4%)
  matrix products  47.9 us (3%)
  blocking collectives  23.8 us (2%)
    all_gather x1, waiting for transfers between devices, shards(): lax.all_gather(local_grad, ('row', 'col'))  728 us
    psum x1, waiting for transfers between devices, shards(): pre = lax.psum(partial_value, 'col')  276 us
    reduce_scatter x1, waiting for transfers between devices, shards(): lax.psum_scatter(back_partial, 'row', scatter_dimension=0, tiled=True)  189 us
    scatter-add x3, other arithmetic, one_block(): return totals.at[column_part].add(products)  55.9 us
    scatter-add x3, other arithmetic, one_block(): return totals.at[row_part].add(products)  55.4 us
    all_gather x1, waiting for transfers between devices, shards(): hidden_columns = lax.all_gather(hidden, 'row', axis=0, tiled=True)  49.4 us
    reduce_sum x1, other arithmetic, shards(): jnp.sum(lax.all_gather(local_grad, ('row', 'col')), axis=0)  40.6 us
  transfers between devices with their start and end apart: 4, of which 4 were waited for; matrix products, arithmetic and copies ran while one was open for 1% of the time, Pallas kernels for 0%

profile of v1, /device:TPU:1, one launch (start us, length us, event | category | flops | bytes accessed | tf_op | source)
XLA Modules:
  0.0 1557.0 jit_solution(8667831033002635478)
XLA Ops:
  13.9 23.8 %all_to_all.5 = bf16[128,4,512]{2,1,0:T(4,128)(2,1)S(1)} all-to-all(bf16[128,4,512]{2,1,0:T(4,128)(2,1)S(1)} %reshape.48), channel_id=1, replica_groups=mesh['row'=16,'col'=8] {'row','col'}, dimensions={0} | all-to-all | bytes 1048576 | tf_op jit(solution)/shard_map/all_to_all | solution.py:19
  41.1 49.4 %all-gather.4.cloned.1.call-done = bf16[8192,512]{1,0:T(8,128)(2,1)} async-done(((bf16[512,512]{1,0:T(8,128)(2,1)}), bf16[8192,512]{1,0:T(8,128)(2,1)}) %all-gather.4.cloned.1.call-update) | async-done | bytes 8388624 | tf_op jit(solution)/shard_map/all_gather | solution.py:68
  94.8 97.2 %while.20 = (s32[]{:T(128)}, f32[32,128,512]{2,1,0:T(8,128)}, s32[]{:T(128)}, s32[192]{0:T(256)S(1)}, s32[]{:T(128)}, /*index=5*/bf16[192,128,128]{2,1,0:T(8,128...) while((s32[]{:T(128)}, f32[32,128,512]{2,1,0:T(8,128)}, ...), condition=%wide.region_3.4_spmd, body=%wide.region_1.3_spmd.sunk | while | flops 539493632 | bytes 47191152 | solution.py:49
  95.6 6.2 gather_fusion
  101.7 7.0 fusion.29
  108.8 18.7 %scatter_fusion = f32[32,128,512]{2,1,0:T(8,128)} fusion(f32[32,128,512]{2,1,0:T(8,128)} %get-tuple-element.257, s32[32]{0:T(128)S(1)} %get-tuple-element.232, f32[32,128,512]{2,1,0:T(8,128)} %fusion.29), kind=kCustom, calls=%fused_computation.3.clone.1 | custom fusion | flops 2097152 | bytes 25165952 | tf_op jit(solution)/shard_map/while/body/scatter-add | solution.py:42
  134.4 7.0 fusion.29
  141.4 18.6 %scatter_fusion = f32[32,128,512]{2,1,0:T(8,128)} fusion(f32[32,128,512]{2,1,0:T(8,128)} %get-tuple-element.257, s32[32]{0:T(128)S(1)} %get-tuple-element.232, f32[32,128,512]{2,1,0:T(8,128)} %fusion.29), kind=kCustom, calls=%fused_computation.3.clone.1 | custom fusion | flops 2097152 | bytes 25165952 | tf_op jit(solution)/shard_map/while/body/scatter-add | solution.py:42
  166.9 7.0 fusion.29
  173.9 18.1 %scatter_fusion = f32[32,128,512]{2,1,0:T(8,128)} fusion(f32[32,128,512]{2,1,0:T(8,128)} %get-tuple-element.257, s32[32]{0:T(128)S(1)} %get-tuple-element.232, f32[32,128,512]{2,1,0:T(8,128)} %fusion.29), kind=kCustom, calls=%fused_computation.3.clone.1 | custom fusion | flops 2097152 | bytes 25165952 | tf_op jit(solution)/shard_map/while/body/scatter-add | solution.py:42
  192.1 8.6 copy.10
  200.6 275.6 %all-reduce.2.cloned.1.call-done = f32[4096,512]{1,0:T(8,128)} async-done(((f32[4096,512]{1,0:T(8,128)}), f32[4096,512]{1,0:T(8,128)}) %all-reduce.2.cloned.1.call-update) | async-done | bytes 8388624 | tf_op jit(solution)/shard_map/psum | solution.py:73
  476.3 7.6 multiply_convert_fusion
  483.9 7.9 broadcast_in_dim.38
  491.7 94.1 %while.21 = (s32[]{:T(128)}, f32[64,128,512]{2,1,0:T(8,128)}, s32[]{:T(128)}, s32[192]{0:T(256)S(1)}, s32[]{:T(128)}, /*index=5*/bf16[192,128,128]{1,2,0:T(8,128...) while((s32[]{:T(128)}, f32[64,128,512]{2,1,0:T(8,128)}, ...), condition=%wide.region_7.8_spmd, body=%wide.region_5.7_spmd.sunk | while | flops 539493632 | bytes 47191152 | solution.py:49
  497.5 7.0 fusion.32
  504.5 18.6 %scatter_fusion.1 = f32[64,128,512]{2,1,0:T(8,128)} fusion(f32[64,128,512]{2,1,0:T(8,128)} %get-tuple-element.293, s32[32]{0:T(128)S(1)} %get-tuple-element.242, f32[32,128,512]{2,1,0:T(8,128)} %fusion.32), kind=kCustom, calls=%fused_computation.4.clone.1 | custom fusion | flops 2097152 | bytes 25165952 | tf_op jit(solution)/shard_map/while/body/scatter-add | solution.py:47
  528.8 7.0 fusion.32
  535.8 18.6 %scatter_fusion.1 = f32[64,128,512]{2,1,0:T(8,128)} fusion(f32[64,128,512]{2,1,0:T(8,128)} %get-tuple-element.293, s32[32]{0:T(128)S(1)} %get-tuple-element.242, f32[32,128,512]{2,1,0:T(8,128)} %fusion.32), kind=kCustom, calls=%fused_computation.4.clone.1 | custom fusion | flops 2097152 | bytes 25165952 | tf_op jit(solution)/shard_map/while/body/scatter-add | solution.py:47
  560.1 7.0 fusion.32
  567.2 18.7 %scatter_fusion.1 = f32[64,128,512]{2,1,0:T(8,128)} fusion(f32[64,128,512]{2,1,0:T(8,128)} %get-tuple-element.293, s32[32]{0:T(128)S(1)} %get-tuple-element.242, f32[32,128,512]{2,1,0:T(8,128)} %fusion.32), kind=kCustom, calls=%fused_computation.4.clone.1 | custom fusion | flops 2097152 | bytes 25165952 | tf_op jit(solution)/shard_map/while/body/scatter-add | solution.py:47
  586.0 188.7 %reduce-scatter.2.cloned.1.call-done = f32[512,512]{1,0:T(8,128)} async-done(((f32[8192,512]{1,0:T(8,128)}), f32[512,512]{1,0:T(8,128)}) %reduce-scatter.2.cloned.1.call-update) | async-done | bytes 1048592 | tf_op jit(solution)/shard_map/reduce_scatter | solution.py:80
  780.3 728.5 %all-gather.6.cloned.1.call-done = f32[65536,512]{1,0:T(8,128)} async-done(((f32[512,512]{1,0:T(8,128)}), f32[65536,512]{1,0:T(8,128)}) %all-gather.6.cloned.1.call-update) | async-done | bytes 134217744 | tf_op jit(solution)/shard_map/all_gather | solution.py:87
  1508.8 40.6 %reduce_sum.9 = f32[512,512]{1,0:T(8,128)S(1)} reduce(f32[128,512,512]{2,1,0:T(8,128)} %bitcast.9, f32[]{:T(128)} %constant.36.clone.1), dimensions={0}, to_apply=%region_9.10 | reduce | flops 33292288 | bytes 135266304 | tf_op jit(solution)/shard_map/reduce_sum | solution.py:87
  (55 shorter events, 52.0 us)
Async XLA Ops:
  7.2 4.6 copy-start
  7.2 83.3 %all-gather.4.cloned.1.call-start = ((), (), s32[]{:S(2)}) async-start(), calls=%async_computation.2 | async-start | bytes 8912896 | tf_op jit(solution)/shard_map/all_gather | solution.py:68
  11.7 83.0 %copy-start.4 = (s32[1,1,192]{2,1,0:T(1,128)S(1)}, s32[1,1,192]{2,1,0:T(1,128)}, u32[]{:S(2)}) copy-start(s32[1,1,192]{2,1,0:T(1,128)} %param.16) | copy-start | bytes 2308
  11.8 83.0 %copy-start.5 = (s32[1,1,192]{2,1,0:T(1,128)S(1)}, s32[1,1,192]{2,1,0:T(1,128)}, u32[]{:S(2)}) copy-start(s32[1,1,192]{2,1,0:T(1,128)} %param.17) | copy-start | bytes 2308
  37.9 56.9 %copy-start.2 = (bf16[512,512]{1,0:T(8,128)(2,1)}, bf16[512,512]{1,0:T(8,128)(2,1)S(1)}, u32[]{:S(2)}) copy-start(bf16[512,512]{1,0:T(8,128)(2,1)S(1)} %reshape.49) | copy-start | bytes 1572868
  40.4 435.9 %all-reduce.2.cloned.1.call-start = ((), (), s32[]{:S(2)}) async-start(), calls=%async_computation.3 | async-start | bytes 16777216 | tf_op jit(solution)/shard_map/psum | solution.py:73
  192.0 582.7 %reduce-scatter.2.cloned.1.call-start = ((), (), s32[]{:S(2)}) async-start(), calls=%async_computation.4 | async-start | bytes 17825792 | tf_op jit(solution)/shard_map/reduce_scatter | solution.py:80
  585.9 188.8 %copy-start.3 = (bf16[512,512]{1,0:T(8,128)(2,1)S(1)}, bf16[512,512]{1,0:T(8,128)(2,1)}, u32[]{:S(2)}) copy-start(bf16[512,512]{1,0:T(8,128)(2,1)} %copy-done.2) | copy-start | bytes 1572868
  585.9 922.9 %all-gather.6.cloned.1.call-start = ((), (), s32[]{:S(2)}) async-start(), calls=%async_computation.5 | async-start | bytes 135266304 | tf_op jit(solution)/shard_map/all_gather | solution.py:87
  1508.8 41.6 %copy-start.1 = (bf16[512,512]{1,0:T(8,128)(2,1)S(1)}, bf16[512,512]{1,0:T(8,128)(2,1)}, u32[]{:S(2)}) copy-start(bf16[512,512]{1,0:T(8,128)(2,1)} %param.12) | copy-start | bytes 1572868
Sparse Core Ops, SparseCore 0:
  40.5 49.9 all-gather.3
  192.1 284.1 all-reduce.1
  586.0 188.6 reduce-scatter.1
  778.1 730.6 all-gather.5
